TPU v7x, 512 devices: a whole 4x8x8 slice. The times are simulated.
512 devices in a mesh: gal: 64 (over x, z, core), pix: 8 (over y).
Axes of the slice: x: 4, y: 8, z: 8, core: 2. Of those that a mesh axis runs over, the one named last changes fastest.
Arguments:
- spectra: bfloat16 [32768, 8192], P('gal', 'pix'), may hold values from -500 to 500
- sketch: bfloat16 [32768, 128], P('gal'), may hold values from -0.25 to 0.25
- block_mask: int32 [64, 64], P('gal', 'pix'), may hold values from 0 to 1, as said below
- rank_key: int32 [64], P('gal'), may hold values from 0 to 63, each once
Outputs:
- projector_basis: float32 [8192, 128], P('pix')
- scores: float32 [32768, 128], P('gal')
Inputs may be any that keep to these rules, and one draw needn't show every extreme that they name: `block_mask`: in every galaxy batch at least half of the 64 blocks are valid.
All inputs are finite; a program needn't handle non-finite values.
Results may differ from a plain program's by a relative error of at most 0.0059.
Values sent between devices are 32-bit elements; how exact they have to be, the bound alone decides.
No kernel may reach another device: no remote copies, remote signals or barrier semaphores. Data moves between devices by JAX's collectives and lax.ppermute only.
A program may use at most 64 MiB of HBM per device.

v0:
```python
import math
import jax
import jax.numpy as jnp
from jax import lax
from jax.sharding import PartitionSpec as P

NPIX = 8192
K = 128
ITERS = 2


def swapped(block, axis, bit):
    count = lax.axis_size(axis)
    route = []
    for low in range(count):
        high = low | 1 << bit
        if high != low and high < count:
            route += [(low, high), (high, low)]
    return lax.ppermute(block, axis, route)


def gram_of(left_side, right_side):
    return lax.dot_general(
        left_side,
        right_side,
        (((0,), (0,)), ((), ())),
        precision=lax.Precision.HIGHEST,
        preferred_element_type=jnp.float32,
    )


def matmul_high(left_side, right_side):
    return jnp.dot(
        left_side, right_side, precision=lax.Precision.HIGHEST, preferred_element_type=jnp.float32
    )


def orthonormal(columns, gram_matrix):
    lower_factor = jnp.linalg.cholesky(gram_matrix)
    return lax.linalg.triangular_solve(
        lower_factor, columns, left_side=False, lower=True, transpose_a=True
    )


def rotate(gram_matrix):
    rotation = jnp.concatenate(
        [jnp.eye(K, dtype=jnp.float32), jnp.zeros((K, K), jnp.float32)], axis=0
    )
    for iteration in range(ITERS):
        mapped = matmul_high(gram_matrix, rotation)
        rotation = orthonormal(mapped, gram_of(mapped, mapped))
    return rotation


def per_device(spectra, sketch, block_mask, rank_key):
    pixel_width = spectra.shape[1]
    pixel_mask = jnp.repeat(block_mask[0], pixel_width // block_mask.shape[1]).astype(jnp.bfloat16)
    masked = spectra * pixel_mask[None, :]
    sketched = lax.dot_general(
        masked, sketch, (((0,), (0,)), ((), ())), preferred_element_type=jnp.float32
    )
    gram_sum = lax.psum(gram_of(sketched, sketched), "pix")
    ortho_panel = orthonormal(sketched, gram_sum)
    ortho_half = ortho_panel.astype(jnp.bfloat16)
    projected = lax.psum(jnp.dot(masked, ortho_half, preferred_element_type=jnp.float32), "pix")
    covariance = gram_of(projected, projected)
    factor = jnp.linalg.cholesky(covariance)
    panel_now = matmul_high(ortho_panel, factor)
    own_gram = gram_of(factor, factor)
    all_keys = lax.all_gather(rank_key, "gal", axis=0, tiled=True)
    position = lax.axis_index("gal")
    level_count = lax.axis_size("gal").bit_length() - 1
    for section in range(level_count):
        block_span = 2**section
        group_min = jnp.min(all_keys.reshape(-1, block_span), axis=1)
        my_group = position // block_span
        own_min = group_min[my_group]
        other_min = group_min[jnp.bitwise_xor(my_group, 1)]
        lead_flag = own_min < other_min
        partner = swapped(panel_now, "gal", section)
        front_panel = jnp.where(lead_flag, panel_now, partner)
        back_panel = jnp.where(lead_flag, partner, panel_now)
        joined = jnp.concatenate([front_panel, back_panel], axis=1)
        gram_matrix = lax.psum(gram_of(joined, joined), "pix")
        rotation = rotate(gram_matrix)
        panel_now = matmul_high(joined, rotation)
        own_gram = gram_of(rotation, matmul_high(gram_matrix, rotation))
    projector_basis = orthonormal(panel_now, own_gram) * math.sqrt(NPIX)
    basis_half = projector_basis.astype(jnp.bfloat16)
    score_terms = jnp.dot(masked, basis_half, preferred_element_type=jnp.float32)
    scores = lax.psum(score_terms, "pix") / NPIX
    return (projector_basis, scores)


def solution(mesh):
    in_specs = (P("gal", "pix"), P("gal", None), P("gal", "pix"), P("gal"))
    out_specs = (P("pix", None), P("gal", None))
    return jax.shard_map(
        per_device, mesh=mesh, in_specs=in_specs, out_specs=out_specs, check_vma=False
    )
```

profile of v0, /device:TPU:2, one launch (start us, length us, event | category | flops | bytes accessed | tf_op | source)
XLA Modules:
  0.0 1212.3 jit_solution(16196803938518872094)
XLA Ops:
  8.1 1.7 fusion.17
  9.8 1.6 fusion.140
  11.5 81.2 %all-reduce.12.cloned.1.call-done = f32[128,128]{0,1:T(8,128)} async-done(((f32[128,128]{0,1:T(8,128)}), f32[128,128]{0,1:T(8,128)}) %all-reduce.12.cloned.1.call-update) | async-done | bytes 65552 | tf_op jit(solution)/shard_map/psum | solution.py:62
  94.5 11.7 cholesky.239
  107.6 9.8 custom-call.20
  119.5 76.4 %all-reduce.14.cloned.1.call-done = f32[512,128]{1,0:T(8,128)} async-done(((f32[512,128]{1,0:T(8,128)}), f32[512,128]{1,0:T(8,128)}) %all-reduce.14.cloned.1.call-update) | async-done | bytes 262160 | tf_op jit(solution)/shard_map/psum | solution.py:65
  195.9 1.6 fusion.141
  197.6 11.7 cholesky.250
  210.0 1.3 fusion.80
  211.3 1.9 collective-permute-start
  213.9 1.3 dynamic-slice.6
  215.9 20.6 %all-reduce.1 = s32[64]{0:T(128)S(1)} all-reduce(s32[64]{0:T(128)S(1)} %dynamic-update-slice.2), channel_id=1, replica_groups=mesh['gal'=64,'pix'=8] {'gal'}, use_global_device_ids=true, to_apply=%add.1 | all-reduce | flops 64 | bytes 512
  238.5 1.7 fusion.12
  240.7 71.8 %all-reduce.16.cloned.1.call-done = f32[256,256]{1,0:T(8,128)} async-done(((f32[256,256]{1,0:T(8,128)}), f32[256,256]{1,0:T(8,128)}) %all-reduce.16.cloned.1.call-update) | async-done | bytes 262160 | tf_op jit(solution)/shard_map/psum | solution.py:84
  314.2 11.7 cholesky.261
  327.2 9.8 custom-call.21
  338.3 11.7 cholesky.272
  351.3 21.1 %custom-call.22 = f32[1,128,128]{1,2,0:T(8,128)S(1)} custom-call(f32[1,128,128]{2,1,0:T(8,128)S(1)} %fusion.38), custom_call_target="InvertDiagBlocksLowerTriangular" | custom-call | tf_op jit(solution)/shard_map/triangular_solve/custom-call.2 | solution.py:40
  373.5 3.6 collective-permute-start.1
  379.2 5.4 collective-permute-done.1
  384.6 1.7 fusion.10
  386.4 76.7 %all-reduce.18.cloned.1.call-done = f32[256,256]{1,0:T(8,128)} async-done(((f32[256,256]{1,0:T(8,128)}), f32[256,256]{1,0:T(8,128)}) %all-reduce.18.cloned.1.call-update) | async-done | bytes 262160 | tf_op jit(solution)/shard_map/psum | solution.py:84
  463.2 1.2 fusion.30
  464.9 11.7 cholesky.283
  477.9 9.8 custom-call.23
  489.0 11.7 cholesky.294
  502.0 10.2 custom-call.24
  513.3 4.6 collective-permute-start.2
  520.0 16.3 %collective-permute-done.2 = f32[1024,128]{0,1:T(8,128)S(1)} collective-permute-done((f32[1024,128]{0,1:T(8,128)S(1)}, f32[1024,128]{0,1:T(8,128)S(1)}, u32[]{:S(2)}, u32[]{:S(2)}) %collective-permute-start.2) | collective-permute-done | bytes 524320 | tf_op jit(solution)/shard_map/ppermute | solution.py:19
  536.4 1.7 fusion.8
  538.2 76.9 %all-reduce.20.cloned.1.call-done = f32[256,256]{1,0:T(8,128)} async-done(((f32[256,256]{1,0:T(8,128)}), f32[256,256]{1,0:T(8,128)}) %all-reduce.20.cloned.1.call-update) | async-done | bytes 262160 | tf_op jit(solution)/shard_map/psum | solution.py:84
  616.8 11.7 cholesky.305
  629.9 9.8 custom-call.25
  640.9 11.7 cholesky.316
  654.0 10.0 custom-call.26
  665.0 8.0 collective-permute-start.3
  675.1 15.5 %collective-permute-done.3 = f32[1024,128]{0,1:T(8,128)S(1)} collective-permute-done((f32[1024,128]{0,1:T(8,128)S(1)}, f32[1024,128]{0,1:T(8,128)S(1)}, u32[]{:S(2)}, u32[]{:S(2)}) %collective-permute-start.3) | collective-permute-done | bytes 524320 | tf_op jit(solution)/shard_map/ppermute | solution.py:19
  690.7 1.7 fusion.6
  692.5 77.3 %all-reduce.22.cloned.1.call-done = f32[256,256]{1,0:T(8,128)} async-done(((f32[256,256]{1,0:T(8,128)}), f32[256,256]{1,0:T(8,128)}) %all-reduce.22.cloned.1.call-update) | async-done | bytes 262160 | tf_op jit(solution)/shard_map/psum | solution.py:84
  771.5 11.7 cholesky.327
  784.6 9.8 custom-call.27
  795.6 11.7 cholesky.338
  808.6 10.2 custom-call.28
  819.9 2.5 collective-permute-start.4
  824.5 6.5 collective-permute-done.4
  831.0 1.7 fusion.4
  832.9 76.7 %all-reduce.24.cloned.1.call-done = f32[256,256]{1,0:T(8,128)} async-done(((f32[256,256]{1,0:T(8,128)}), f32[256,256]{1,0:T(8,128)}) %all-reduce.24.cloned.1.call-update) | async-done | bytes 262160 | tf_op jit(solution)/shard_map/psum | solution.py:84
  911.3 11.7 cholesky.349
  924.4 9.8 custom-call.29
  935.4 11.7 cholesky.360
  948.5 10.0 custom-call.30
  959.4 4.0 collective-permute-start.5
  965.6 6.5 collective-permute-done.5
  972.1 1.7 fusion.2
  973.9 76.7 %all-reduce.26.cloned.1.call-done = f32[256,256]{1,0:T(8,128)} async-done(((f32[256,256]{1,0:T(8,128)}), f32[256,256]{1,0:T(8,128)}) %all-reduce.26.cloned.1.call-update) | async-done | bytes 262160 | tf_op jit(solution)/shard_map/psum | solution.py:84
  1052.4 11.7 cholesky.371
  1065.4 9.8 custom-call.31
  1076.5 11.7 cholesky.382
  1089.5 10.0 custom-call.32
  1099.9 1.8 fusion.1
  1102.5 11.7 cholesky.393
  1115.5 9.8 custom-call.33
  1128.1 75.6 %all-reduce.28.cloned.1.call-done = f32[512,128]{1,0:T(8,128)} async-done(((f32[512,128]{1,0:T(8,128)}), f32[512,128]{1,0:T(8,128)}) %all-reduce.28.cloned.1.call-update) | async-done | bytes 262160 | tf_op jit(solution)/shard_map/psum | solution.py:91
  1203.7 1.7 broadcast_multiply_fusion
  (183 shorter events, 55.8 us)
Async XLA Ops:
  7.2 0.9 copy-start
  7.2 85.5 %all-reduce.12.cloned.1.call-start = ((), (), s32[]{:S(2)}) async-start(), calls=%async_computation | async-start | bytes 131072 | tf_op jit(solution)/shard_map/psum | solution.py:62
  11.4 106.6 %copy-start.1 = (bf16[512,1024]{1,0:T(8,128)(2,1)S(1)}, bf16[512,1024]{1,0:T(8,128)(2,1)}, u32[]{:S(2)}) copy-start(bf16[512,1024]{1,0:T(8,128)(2,1)} %param.9) | copy-start | bytes 3145732
  11.4 184.4 %all-reduce.14.cloned.1.call-start = ((), (), s32[]{:S(2)}) async-start(), calls=%async_computation.1 | async-start | bytes 524288 | tf_op jit(solution)/shard_map/psum | solution.py:65
  119.2 193.3 %all-reduce.16.cloned.1.call-start = ((), (), s32[]{:S(2)}) async-start(), calls=%async_computation.2 | async-start | bytes 524288 | tf_op jit(solution)/shard_map/psum | solution.py:84
  211.3 27.1 %collective-permute-start = (f32[1024,128]{0,1:T(8,128)S(1)}, f32[1024,128]{0,1:T(8,128)S(1)}, u32[]{:S(2)}, u32[]{:S(2)}) collective-permute-start(f32[1024,128]{0,1:T(8,128)S(1)} %fusion.80), channel_id=1, source_target_pairs={{0,8},{8,0},{16,24},{24,16},{32,40},{40,32},{48,56},{56,48},{64,72... | collective-permute-start | bytes 1572872 | tf_op jit(solution)/shard_map/ppermute | solution.py:19
  240.3 222.9 %all-reduce.18.cloned.1.call-start = ((), (), s32[]{:S(2)}) async-start(), calls=%async_computation.3 | async-start | bytes 524288 | tf_op jit(solution)/shard_map/psum | solution.py:84
  325.9 11.5 copy-start.3
  373.5 11.1 collective-permute-start.1
  386.4 228.7 %all-reduce.20.cloned.1.call-start = ((), (), s32[]{:S(2)}) async-start(), calls=%async_computation.4 | async-start | bytes 524288 | tf_op jit(solution)/shard_map/psum | solution.py:84
  476.6 11.5 copy-start.4
  513.3 23.1 %collective-permute-start.2 = (f32[1024,128]{0,1:T(8,128)S(1)}, f32[1024,128]{0,1:T(8,128)S(1)}, u32[]{:S(2)}, u32[]{:S(2)}) collective-permute-start(f32[1024,128]{0,1:T(8,128)S(1)} %fusion.9), channel_id=1, source_target_pairs={{0,32},{32,0},{8,40},{40,8},{16,48},{48,16},{24,56},{56,24},{64,96... | collective-permute-start | bytes 1572872 | tf_op jit(solution)/shard_map/ppermute | solution.py:19
  538.2 231.6 %all-reduce.22.cloned.1.call-start = ((), (), s32[]{:S(2)}) async-start(), calls=%async_computation.5 | async-start | bytes 524288 | tf_op jit(solution)/shard_map/psum | solution.py:84
  628.6 11.5 copy-start.5
  665.0 25.6 %collective-permute-start.3 = (f32[1024,128]{0,1:T(8,128)S(1)}, f32[1024,128]{0,1:T(8,128)S(1)}, u32[]{:S(2)}, u32[]{:S(2)}) collective-permute-start(f32[1024,128]{0,1:T(8,128)S(1)} %fusion.7), channel_id=1, source_target_pairs={{0,64},{64,0},{8,72},{72,8},{16,80},{80,16},{24,88},{88,24},{32,96... | collective-permute-start | bytes 1572872 | tf_op jit(solution)/shard_map/ppermute | solution.py:19
  692.5 217.1 %all-reduce.24.cloned.1.call-start = ((), (), s32[]{:S(2)}) async-start(), calls=%async_computation.6 | async-start | bytes 524288 | tf_op jit(solution)/shard_map/psum | solution.py:84
  783.2 11.5 copy-start.6
  819.9 11.1 collective-permute-start.4
  832.8 217.9 %all-reduce.26.cloned.1.call-start = ((), (), s32[]{:S(2)}) async-start(), calls=%async_computation.7 | async-start | bytes 524288 | tf_op jit(solution)/shard_map/psum | solution.py:84
  923.0 11.5 copy-start.7
  959.4 12.6 %collective-permute-start.5 = (f32[1024,128]{0,1:T(8,128)S(1)}, f32[1024,128]{0,1:T(8,128)S(1)}, u32[]{:S(2)}, u32[]{:S(2)}) collective-permute-start(f32[1024,128]{0,1:T(8,128)S(1)} %fusion.3), channel_id=1, source_target_pairs={{0,256},{256,0},{8,264},{264,8},{16,272},{272,16},{24,280},{280,24... | collective-permute-start | bytes 1572872 | tf_op jit(solution)/shard_map/ppermute | solution.py:19
  973.9 229.8 %all-reduce.28.cloned.1.call-start = ((), (), s32[]{:S(2)}) async-start(), calls=%async_computation.8 | async-start | bytes 524288 | tf_op jit(solution)/shard_map/psum | solution.py:91
  1064.1 11.5 copy-start.2
Sparse Core Ops, SparseCore 0:
  11.6 81.1 all-reduce.11
  119.3 76.4 all-reduce.13
  240.4 71.9 all-reduce.15
  386.5 76.6 all-reduce.17
  538.3 76.7 all-reduce.19
  692.6 77.1 all-reduce.21
  832.9 76.6 all-reduce.23
  974.0 76.6 all-reduce.25
  1127.3 76.4 all-reduce.27
where the time goes:
time: 1220 us; the launch traced here: 1210 us
  waiting for transfers between devices  740 us (61%)
  other arithmetic  349 us (29%)
  matrix products  44 us (4%)
  starting transfers between devices  25.5 us (2%)
  between operations  23.8 us (2%)
  blocking collectives  20.6 us (2%)
    psum x6, waiting for transfers between devices, per_device(): gram_matrix = lax.psum(gram_of(joined, joined), 'pix')  456 us
    another operation x43, other arithmetic, orthonormal(): lower_factor = jnp.linalg.cholesky(gram_matrix)  173 us
    another operation x28, other arithmetic, orthonormal(): lax.linalg.triangular_solve(lower_factor, columns, left_side=False, lower...  159 us
    psum x1, waiting for transfers between devices, per_device(): gram_sum = lax.psum(gram_of(sketched, sketched), 'pix')  81.2 us
    psum x1, waiting for transfers between devices, per_device(): lax.psum(jnp.dot(masked, ortho_half, preferred_element_type=jnp.float32),...  76.4 us
    psum x1, waiting for transfers between devices, per_device(): scores = lax.psum(score_terms, 'pix') / NPIX  75.6 us
    ppermute x6, waiting for transfers between devices, swapped(): return lax.ppermute(block, axis, route)  50.1 us
    ppermute x6, starting transfers between devices, swapped(): return lax.ppermute(block, axis, route)  24.6 us
  transfers between devices with their start and end apart: 15, of which 14 were waited for; matrix products, arithmetic and copies ran while one was open for 1% of the time, Pallas kernels for 0%

commit v1 on v0

--- a/solution.py
+++ b/solution.py
@@ -7,6 +7,12 @@
 NPIX = 8192
 K = 128
 ITERS = 2
+
+
+def gather_and_add(block, name):
+    terms = lax.all_gather(block, name, axis=0, tiled=False)
+    summed = terms.sum(axis=0)
+    return summed
 
 
 def swapped(block, axis, bit):
@@ -81,7 +87,7 @@
         front_panel = jnp.where(lead_flag, panel_now, partner)
         back_panel = jnp.where(lead_flag, partner, panel_now)
         joined = jnp.concatenate([front_panel, back_panel], axis=1)
-        gram_matrix = lax.psum(gram_of(joined, joined), "pix")
+        gram_matrix = gather_and_add(gram_of(joined, joined), "pix")
         rotation = rotate(gram_matrix)
         panel_now = matmul_high(joined, rotation)
         own_gram = gram_of(rotation, matmul_high(gram_matrix, rotation))

time: 1220 us -> 1020 us (0.84)
  waiting for transfers between devices: 740 us -> 539 us
    psum x6 -> x0, waiting for transfers between devices: 456 us -> none  [per_device(): gram_matrix = lax.psum(gram_of(joined, joined), 'pix')]
    all_gather x0 -> x6, waiting for transfers between devices: none -> 250 us  [gather_and_add(): terms = lax.all_gather(block, name, axis=0, tiled=False)]
where the time goes in v1:
time: 1020 us
  waiting for transfers between devices  539 us (53%)
  other arithmetic  360 us (35%)
  matrix products  38.4 us (4%)
  starting transfers between devices  25.5 us (2%)
  between operations  23.8 us (2%)
  blocking collectives  20.6 us (2%)
    all_gather x6, waiting for transfers between devices, gather_and_add(): terms = lax.all_gather(block, name, axis=0, tiled=False)  250 us
    another operation x43, other arithmetic, orthonormal(): lower_factor = jnp.linalg.cholesky(gram_matrix)  173 us
    another operation x28, other arithmetic, orthonormal(): lax.linalg.triangular_solve(lower_factor, columns, left_side=False, lower...  159 us
    psum x1, waiting for transfers between devices, per_device(): gram_sum = lax.psum(gram_of(sketched, sketched), 'pix')  81.2 us
    psum x1, waiting for transfers between devices, per_device(): lax.psum(jnp.dot(masked, ortho_half, preferred_element_type=jnp.float32),...  76.4 us
    psum x1, waiting for transfers between devices, per_device(): scores = lax.psum(score_terms, 'pix') / NPIX  76 us
    ppermute x6, waiting for transfers between devices, swapped(): return lax.ppermute(block, axis, route)  54.8 us
    ppermute x6, starting transfers between devices, swapped(): return lax.ppermute(block, axis, route)  24.6 us
  transfers between devices with their start and end apart: 15, of which 14 were waited for; matrix products, arithmetic and copies ran while one was open for 1% of the time, Pallas kernels for 0%

profile of v1, /device:TPU:2, one launch (start us, length us, event | category | flops | bytes accessed | tf_op | source)
XLA Modules:
  0.0 1016.8 jit_solution(15229257849456385658)
XLA Ops:
  8.1 1.8 fusion.17
  11.6 81.2 %all-reduce.6.cloned.1.call-done = f32[128,128]{0,1:T(8,128)} async-done(((f32[128,128]{0,1:T(8,128)}), f32[128,128]{0,1:T(8,128)}) %all-reduce.6.cloned.1.call-update) | async-done | bytes 65552 | tf_op jit(solution)/shard_map/psum | solution.py:68
  94.6 11.7 %cholesky.239 = f32[128,128]{1,0:T(8,128)S(1)} custom-call(f32[128,128]{1,0:T(8,128)S(1)} %fusion.78), custom_call_target="Cholesky" | custom-call | tf_op jit(solution)/shard_map/jit(cholesky)/cholesky | solution.py:45
  107.7 9.8 custom-call.20
  119.6 76.4 %all-reduce.8.cloned.1.call-done = f32[512,128]{1,0:T(8,128)} async-done(((f32[512,128]{1,0:T(8,128)}), f32[512,128]{1,0:T(8,128)}) %all-reduce.8.cloned.1.call-update) | async-done | bytes 262160 | tf_op jit(solution)/shard_map/psum | solution.py:71
  197.7 11.7 %cholesky.250 = f32[128,128]{1,0:T(8,128)S(1)} custom-call(f32[128,128]{1,0:T(8,128)S(1)} %fusion.76), custom_call_target="Cholesky" | custom-call | tf_op jit(solution)/shard_map/jit(cholesky)/cholesky | solution.py:73
  211.3 1.9 collective-permute-start
  216.0 20.6 %all-reduce.1 = s32[64]{0:T(128)S(1)} all-reduce(s32[64]{0:T(128)S(1)} %dynamic-update-slice.2), channel_id=1, replica_groups=mesh['gal'=64,'pix'=8] {'gal'}, use_global_device_ids=true, to_apply=%add.1 | all-reduce | flops 64 | bytes 512
  238.6 1.7 fusion.12
  240.8 37.6 %all-gather.13.cloned.1.call-done = f32[2048,256]{1,0:T(8,128)} async-done(((f32[256,256]{1,0:T(8,128)}), f32[2048,256]{1,0:T(8,128)}) %all-gather.13.cloned.1.call-update) | async-done | bytes 2097168 | tf_op jit(solution)/shard_map/all_gather | solution.py:13
  278.4 1.8 reduce_sum.54
  280.9 11.7 %cholesky.261 = f32[128,128]{1,0:T(8,128)S(1)} custom-call(f32[128,128]{1,0:T(8,128)S(1)} %fusion.75), custom_call_target="Cholesky" | custom-call | tf_op jit(solution)/shard_map/jit(cholesky)/cholesky | solution.py:45
  294.0 9.8 custom-call.21
  305.0 11.7 %cholesky.272 = f32[128,128]{1,0:T(8,128)S(1)} custom-call(f32[128,128]{1,0:T(8,128)S(1)} %fusion.73), custom_call_target="Cholesky" | custom-call | tf_op jit(solution)/shard_map/jit(cholesky)/cholesky | solution.py:45
  318.1 21.2 %custom-call.22 = f32[1,128,128]{1,2,0:T(8,128)S(1)} custom-call(f32[1,128,128]{2,1,0:T(8,128)S(1)} %fusion.38), custom_call_target="InvertDiagBlocksLowerTriangular" | custom-call | tf_op jit(solution)/shard_map/triangular_solve/custom-call.2 | solution.py:46
  340.3 3.6 collective-permute-start.1
  346.0 6.2 collective-permute-done.1
  352.3 1.7 fusion.10
  354.1 42.5 %all-gather.15.cloned.1.call-done = f32[2048,256]{1,0:T(8,128)} async-done(((f32[256,256]{1,0:T(8,128)}), f32[2048,256]{1,0:T(8,128)}) %all-gather.15.cloned.1.call-update) | async-done | bytes 2097168 | tf_op jit(solution)/shard_map/all_gather | solution.py:13
  396.7 1.8 reduce_sum.55
  399.2 11.7 %cholesky.283 = f32[128,128]{1,0:T(8,128)S(1)} custom-call(f32[128,128]{1,0:T(8,128)S(1)} %fusion.71), custom_call_target="Cholesky" | custom-call | tf_op jit(solution)/shard_map/jit(cholesky)/cholesky | solution.py:45
  412.2 9.8 custom-call.23
  423.3 11.7 %cholesky.294 = f32[128,128]{1,0:T(8,128)S(1)} custom-call(f32[128,128]{1,0:T(8,128)S(1)} %fusion.69), custom_call_target="Cholesky" | custom-call | tf_op jit(solution)/shard_map/jit(cholesky)/cholesky | solution.py:45
  436.3 10.2 %custom-call.24 = f32[1,128,128]{1,2,0:T(8,128)S(1)} custom-call(f32[1,128,128]{2,1,0:T(8,128)S(1)} %fusion.40), custom_call_target="InvertDiagBlocksLowerTriangular" | custom-call | tf_op jit(solution)/shard_map/triangular_solve/custom-call.2 | solution.py:46
  447.5 4.6 collective-permute-start.2
  454.3 17.4 %collective-permute-done.2 = f32[1024,128]{0,1:T(8,128)S(1)} collective-permute-done((f32[1024,128]{0,1:T(8,128)S(1)}, f32[1024,128]{0,1:T(8,128)S(1)}, u32[]{:S(2)}, u32[]{:S(2)}) %collective-permute-start.2) | collective-permute-done | bytes 524320 | tf_op jit(solution)/shard_map/ppermute | solution.py:25
  471.8 1.7 fusion.8
  473.6 42.4 %all-gather.17.cloned.1.call-done = f32[2048,256]{1,0:T(8,128)} async-done(((f32[256,256]{1,0:T(8,128)}), f32[2048,256]{1,0:T(8,128)}) %all-gather.17.cloned.1.call-update) | async-done | bytes 2097168 | tf_op jit(solution)/shard_map/all_gather | solution.py:13
  516.0 1.8 reduce_sum.56
  518.6 11.7 %cholesky.305 = f32[128,128]{1,0:T(8,128)S(1)} custom-call(f32[128,128]{1,0:T(8,128)S(1)} %fusion.67), custom_call_target="Cholesky" | custom-call | tf_op jit(solution)/shard_map/jit(cholesky)/cholesky | solution.py:45
  531.6 9.8 custom-call.25
  542.6 11.7 %cholesky.316 = f32[128,128]{1,0:T(8,128)S(1)} custom-call(f32[128,128]{1,0:T(8,128)S(1)} %fusion.65), custom_call_target="Cholesky" | custom-call | tf_op jit(solution)/shard_map/jit(cholesky)/cholesky | solution.py:45
  555.7 10.0 custom-call.26
  566.7 8.0 collective-permute-start.3
  576.8 16.6 %collective-permute-done.3 = f32[1024,128]{0,1:T(8,128)S(1)} collective-permute-done((f32[1024,128]{0,1:T(8,128)S(1)}, f32[1024,128]{0,1:T(8,128)S(1)}, u32[]{:S(2)}, u32[]{:S(2)}) %collective-permute-start.3) | collective-permute-done | bytes 524320 | tf_op jit(solution)/shard_map/ppermute | solution.py:25
  593.5 1.7 fusion.6
  595.3 42.8 %all-gather.19.cloned.1.call-done = f32[2048,256]{1,0:T(8,128)} async-done(((f32[256,256]{1,0:T(8,128)}), f32[2048,256]{1,0:T(8,128)}) %all-gather.19.cloned.1.call-update) | async-done | bytes 2097168 | tf_op jit(solution)/shard_map/all_gather | solution.py:13
  638.1 1.8 reduce_sum.57
  640.7 11.7 %cholesky.327 = f32[128,128]{1,0:T(8,128)S(1)} custom-call(f32[128,128]{1,0:T(8,128)S(1)} %fusion.63), custom_call_target="Cholesky" | custom-call | tf_op jit(solution)/shard_map/jit(cholesky)/cholesky | solution.py:45
  653.7 9.8 custom-call.27
  664.7 11.7 %cholesky.338 = f32[128,128]{1,0:T(8,128)S(1)} custom-call(f32[128,128]{1,0:T(8,128)S(1)} %fusion.61), custom_call_target="Cholesky" | custom-call | tf_op jit(solution)/shard_map/jit(cholesky)/cholesky | solution.py:45
  677.8 10.2 %custom-call.28 = f32[1,128,128]{1,2,0:T(8,128)S(1)} custom-call(f32[1,128,128]{2,1,0:T(8,128)S(1)} %fusion.44), custom_call_target="InvertDiagBlocksLowerTriangular" | custom-call | tf_op jit(solution)/shard_map/triangular_solve/custom-call.2 | solution.py:46
  689.0 2.5 collective-permute-start.4
  693.6 7.3 collective-permute-done.4
  701.0 1.7 fusion.4
  702.9 42.5 %all-gather.21.cloned.1.call-done = f32[2048,256]{1,0:T(8,128)} async-done(((f32[256,256]{1,0:T(8,128)}), f32[2048,256]{1,0:T(8,128)}) %all-gather.21.cloned.1.call-update) | async-done | bytes 2097168 | tf_op jit(solution)/shard_map/all_gather | solution.py:13
  745.4 1.8 reduce_sum.58
  747.9 11.7 %cholesky.349 = f32[128,128]{1,0:T(8,128)S(1)} custom-call(f32[128,128]{1,0:T(8,128)S(1)} %fusion.59), custom_call_target="Cholesky" | custom-call | tf_op jit(solution)/shard_map/jit(cholesky)/cholesky | solution.py:45
  761.0 9.8 custom-call.29
  772.0 11.7 %cholesky.360 = f32[128,128]{1,0:T(8,128)S(1)} custom-call(f32[128,128]{1,0:T(8,128)S(1)} %fusion.57), custom_call_target="Cholesky" | custom-call | tf_op jit(solution)/shard_map/jit(cholesky)/cholesky | solution.py:45
  785.0 9.9 custom-call.30
  796.0 4.0 collective-permute-start.5
  802.2 7.3 collective-permute-done.5
  809.6 1.7 fusion.2
  811.4 42.5 %all-gather.23.cloned.1.call-done = f32[2048,256]{1,0:T(8,128)} async-done(((f32[256,256]{1,0:T(8,128)}), f32[2048,256]{1,0:T(8,128)}) %all-gather.23.cloned.1.call-update) | async-done | bytes 2097168 | tf_op jit(solution)/shard_map/all_gather | solution.py:13
  853.9 1.8 reduce_sum.59
  856.4 11.7 %cholesky.371 = f32[128,128]{1,0:T(8,128)S(1)} custom-call(f32[128,128]{1,0:T(8,128)S(1)} %fusion.55), custom_call_target="Cholesky" | custom-call | tf_op jit(solution)/shard_map/jit(cholesky)/cholesky | solution.py:45
  869.5 9.8 custom-call.31
  880.5 11.7 %cholesky.382 = f32[128,128]{1,0:T(8,128)S(1)} custom-call(f32[128,128]{1,0:T(8,128)S(1)} %fusion.53), custom_call_target="Cholesky" | custom-call | tf_op jit(solution)/shard_map/jit(cholesky)/cholesky | solution.py:45
  893.6 10.0 custom-call.32
  904.3 1.8 fusion.1
  906.5 11.7 %cholesky.393 = f32[128,128]{1,0:T(8,128)S(1)} custom-call(f32[128,128]{1,0:T(8,128)S(1)} %fusion.51), custom_call_target="Cholesky" | custom-call | tf_op jit(solution)/shard_map/jit(cholesky)/cholesky | solution.py:45
  919.5 9.8 custom-call.33
  932.1 76.0 %all-reduce.10.cloned.1.call-done = f32[512,128]{1,0:T(8,128)} async-done(((f32[512,128]{1,0:T(8,128)}), f32[512,128]{1,0:T(8,128)}) %all-reduce.10.cloned.1.call-update) | async-done | bytes 262160 | tf_op jit(solution)/shard_map/psum | solution.py:97
  (177 shorter events, 58.8 us)
Async XLA Ops:
  7.2 0.9 copy-start
  7.2 85.6 %all-reduce.6.cloned.1.call-start = ((), (), s32[]{:S(2)}) async-start(), calls=%async_computation | async-start | bytes 131072 | tf_op jit(solution)/shard_map/psum | solution.py:68
  8.1 110.0 %copy-start.1 = (bf16[512,1024]{1,0:T(8,128)(2,1)S(1)}, bf16[512,1024]{1,0:T(8,128)(2,1)}, u32[]{:S(2)}) copy-start(bf16[512,1024]{1,0:T(8,128)(2,1)} %param.9) | copy-start | bytes 3145732
  11.5 184.4 %all-reduce.8.cloned.1.call-start = ((), (), s32[]{:S(2)}) async-start(), calls=%async_computation.1 | async-start | bytes 524288 | tf_op jit(solution)/shard_map/psum | solution.py:71
  119.3 159.1 %all-gather.13.cloned.1.call-start = ((), (), s32[]{:S(2)}) async-start(), calls=%async_computation.3 | async-start | bytes 2359296 | tf_op jit(solution)/shard_map/all_gather | solution.py:13
  211.3 27.1 %collective-permute-start = (f32[1024,128]{0,1:T(8,128)S(1)}, f32[1024,128]{0,1:T(8,128)S(1)}, u32[]{:S(2)}, u32[]{:S(2)}) collective-permute-start(f32[1024,128]{0,1:T(8,128)S(1)} %fusion.80), channel_id=1, source_target_pairs={{0,8},{8,0},{16,24},{24,16},{32,40},{40,32},{48,56},{56,48},{64,72... | collective-permute-start | bytes 1572872 | tf_op jit(solution)/shard_map/ppermute | solution.py:25
  240.4 156.3 %all-gather.15.cloned.1.call-start = ((), (), s32[]{:S(2)}) async-start(), calls=%async_computation.4 | async-start | bytes 2359296 | tf_op jit(solution)/shard_map/all_gather | solution.py:13
  340.3 11.9 %collective-permute-start.1 = (f32[1024,128]{0,1:T(8,128)S(1)}, f32[1024,128]{0,1:T(8,128)S(1)}, u32[]{:S(2)}, u32[]{:S(2)}) collective-permute-start(f32[1024,128]{0,1:T(8,128)S(1)} %fusion.11), channel_id=1, source_target_pairs={{0,16},{16,0},{8,24},{24,8},{32,48},{48,32},{40,56},{56,40},{64,80... | collective-permute-start | bytes 1572872 | tf_op jit(solution)/shard_map/ppermute | solution.py:25
  354.1 162.0 %all-gather.17.cloned.1.call-start = ((), (), s32[]{:S(2)}) async-start(), calls=%async_computation.5 | async-start | bytes 2359296 | tf_op jit(solution)/shard_map/all_gather | solution.py:13
  447.5 24.2 %collective-permute-start.2 = (f32[1024,128]{0,1:T(8,128)S(1)}, f32[1024,128]{0,1:T(8,128)S(1)}, u32[]{:S(2)}, u32[]{:S(2)}) collective-permute-start(f32[1024,128]{0,1:T(8,128)S(1)} %fusion.9), channel_id=1, source_target_pairs={{0,32},{32,0},{8,40},{40,8},{16,48},{48,16},{24,56},{56,24},{64,96... | collective-permute-start | bytes 1572872 | tf_op jit(solution)/shard_map/ppermute | solution.py:25
  473.6 164.6 %all-gather.19.cloned.1.call-start = ((), (), s32[]{:S(2)}) async-start(), calls=%async_computation.6 | async-start | bytes 2359296 | tf_op jit(solution)/shard_map/all_gather | solution.py:13
  566.7 26.7 %collective-permute-start.3 = (f32[1024,128]{0,1:T(8,128)S(1)}, f32[1024,128]{0,1:T(8,128)S(1)}, u32[]{:S(2)}, u32[]{:S(2)}) collective-permute-start(f32[1024,128]{0,1:T(8,128)S(1)} %fusion.7), channel_id=1, source_target_pairs={{0,64},{64,0},{8,72},{72,8},{16,80},{80,16},{24,88},{88,24},{32,96... | collective-permute-start | bytes 1572872 | tf_op jit(solution)/shard_map/ppermute | solution.py:25
  595.3 150.1 %all-gather.21.cloned.1.call-start = ((), (), s32[]{:S(2)}) async-start(), calls=%async_computation.7 | async-start | bytes 2359296 | tf_op jit(solution)/shard_map/all_gather | solution.py:13
  689.0 11.9 %collective-permute-start.4 = (f32[1024,128]{0,1:T(8,128)S(1)}, f32[1024,128]{0,1:T(8,128)S(1)}, u32[]{:S(2)}, u32[]{:S(2)}) collective-permute-start(f32[1024,128]{0,1:T(8,128)S(1)} %fusion.5), channel_id=1, source_target_pairs={{0,128},{128,0},{8,136},{136,8},{16,144},{144,16},{24,152},{152,24... | collective-permute-start | bytes 1572872 | tf_op jit(solution)/shard_map/ppermute | solution.py:25
  702.8 151.1 %all-gather.23.cloned.1.call-start = ((), (), s32[]{:S(2)}) async-start(), calls=%async_computation.8 | async-start | bytes 2359296 | tf_op jit(solution)/shard_map/all_gather | solution.py:13
  796.0 13.4 %collective-permute-start.5 = (f32[1024,128]{0,1:T(8,128)S(1)}, f32[1024,128]{0,1:T(8,128)S(1)}, u32[]{:S(2)}, u32[]{:S(2)}) collective-permute-start(f32[1024,128]{0,1:T(8,128)S(1)} %fusion.3), channel_id=1, source_target_pairs={{0,256},{256,0},{8,264},{264,8},{16,272},{272,16},{24,280},{280,24... | collective-permute-start | bytes 1572872 | tf_op jit(solution)/shard_map/ppermute | solution.py:25
  811.3 196.8 %all-reduce.10.cloned.1.call-start = ((), (), s32[]{:S(2)}) async-start(), calls=%async_computation.2 | async-start | bytes 524288 | tf_op jit(solution)/shard_map/psum | solution.py:97
Sparse Core Ops, SparseCore 0:
  11.6 81.1 all-reduce.5
  119.4 76.4 all-reduce.7
  240.5 37.8 all-gather.12
  354.2 42.4 all-gather.14
  473.7 42.3 all-gather.16
  595.4 42.7 all-gather.18
  702.9 42.4 all-gather.20
  811.5 42.4 all-gather.22
  931.3 76.8 all-reduce.9
